TPU v7x, 128 devices: a whole 4x4x4 slice. The times are simulated.
128 devices in a mesh: sky: 16 (over y, z), zb: 8 (over x, core).
Axes of the slice: x: 4, y: 4, z: 4, core: 2. Of those that a mesh axis runs over, the one named last changes fastest.
Arguments:
- stamps: bfloat16 [65536, 5120], P(('sky', 'zb')), may hold values from -6 to 6
- counts: int32 [128], P(('sky', 'zb')), may hold values from 1 to 512, 49152 in all
- dest: int32 [65536, 1], P(('sky', 'zb')), may hold values from 0 to 127; in each aligned block of 512 rows (0 to 511, 512 to 1023, ...) at most 8 rows name the same one
- pixel_ids: int32 [65536], P(('sky', 'zb')), may hold values from 0 to 1023
- conv1_w: bfloat16 [3, 3, 5, 64], replicated, may hold values from -1.25 to 1.25
- conv2_w: bfloat16 [3, 3, 32, 128], replicated, may hold values from -0.5 to 0.5
- conv3_w: bfloat16 [3, 3, 64, 256], replicated, may hold values from -0.375 to 0.375
- dense_w: bfloat16 [4096, 512], replicated, may hold values from -0.125 to 0.125
- head_w: bfloat16 [512, 48], replicated, may hold values from -0.25 to 0.25
Outputs:
- pdf_rows: bfloat16 [131072, 512], P(('sky', 'zb'))
- nz_map: float32 [1024, 512], P('sky', 'zb')
Inputs may be any that keep to these rules, and one draw needn't show every extreme that they name: `dest`: in the rows of one tile owner no worker is named more than 8 times.
All inputs are finite; a program needn't handle non-finite values. No bound on the sum of `counts` on one device may be relied on, other than what follows from the above.
Results may differ from a plain program's by a relative error of at most 0.012.
Values may be sent and summed in bfloat16 or wider, within the bound.
No kernel may reach another device: no remote copies, remote signals or barrier semaphores. Data moves between devices by JAX's collectives and lax.ppermute only.
A program may use at most 384 MiB of HBM per device.

v0:
```python
import math

import jax
import jax.numpy as jnp
from jax import lax
from jax.sharding import PartitionSpec as P

PIX_DEV = 64
NBIN = 512
NCOMP = 16
BANDS = 5
STAMP = 32
GROUPS = 2


Z_TOP = 3.0
SPREAD_LOW = 0.05
SPREAD_RANGE = 0.25


def convolve(images, kernel, groups):
    return lax.conv_general_dilated(
        images,
        kernel,
        (2, 2),
        ((1, 1), (1, 1)),
        dimension_numbers=("NHWC", "HWIO", "NHWC"),
        feature_group_count=groups,
        preferred_element_type=jnp.float32,
    )


def mixture(head_out, bin_total):
    logits = head_out[:, :NCOMP]
    centres = Z_TOP * jax.nn.sigmoid(head_out[:, NCOMP : 2 * NCOMP])
    spreads = SPREAD_LOW + SPREAD_RANGE * jax.nn.sigmoid(head_out[:, 2 * NCOMP :])
    shares = jax.nn.softplus(logits) + 0.1
    shares = shares / jnp.sum(shares, axis=1, keepdims=True)
    bin_edges = Z_TOP * jnp.arange(bin_total + 1, dtype=jnp.float32) / bin_total
    scaled = (bin_edges[None, None, :] - centres[:, :, None]) / (
        spreads[:, :, None] * math.sqrt(2.0)
    )
    cumulative = 0.5 * (1.0 + lax.erf(scaled))
    masses = cumulative[:, :, 1:] - cumulative[:, :, :-1]
    return jnp.sum(shares[:, :, None] * masses, axis=1)


def network(images, conv1_w, conv2_w, conv3_w, dense_w, head_w):
    amount = images.shape[0]
    stamp_grid = images.reshape(amount, STAMP, STAMP, BANDS)
    layer_one = jax.nn.relu(convolve(stamp_grid, conv1_w, 1)).astype(jnp.bfloat16)
    layer_two = jax.nn.relu(convolve(layer_one, conv2_w, GROUPS)).astype(jnp.bfloat16)
    layer_three = jax.nn.relu(convolve(layer_two, conv3_w, GROUPS)).astype(jnp.bfloat16)
    hidden = jax.nn.relu(
        jnp.dot(layer_three.reshape(amount, -1), dense_w, preferred_element_type=jnp.float32)
    ).astype(jnp.bfloat16)
    head_out = jnp.dot(hidden, head_w, preferred_element_type=jnp.float32)
    return mixture(head_out, NBIN)


def local(stamps, counts, dest, pixel_ids, conv1_w, conv2_w, conv3_w, dense_w, head_w):
    devices = lax.axis_size(("sky", "zb"))
    zb_size = lax.axis_size("zb")
    row_total = stamps.shape[0]
    capacity = max(2, 2 * row_total // devices)
    slot_total = devices * capacity
    bin_share = NBIN // zb_size
    row_order = jnp.arange(row_total, dtype=jnp.int32)
    is_valid = row_order < counts[0]
    target = dest[:, 0]
    before = (target[:, None] == target[None, :]) & (row_order[None, :] < row_order[:, None])
    slot_rank = jnp.sum(before.astype(jnp.int32), axis=1)
    position = target * capacity + slot_rank
    tagged = jnp.where(is_valid, pixel_ids, -1)
    pixel_send = jnp.full((slot_total,), -1, jnp.int32).at[position].set(tagged)
    density = network(stamps, conv1_w, conv2_w, conv3_w, dense_w, head_w)
    density = jnp.where(is_valid[:, None], density, 0.0).astype(jnp.bfloat16)
    pdf_send = jnp.zeros((slot_total, NBIN), jnp.bfloat16).at[position].set(density)
    received, labels = (
        lax.all_to_all(
            pdf_send.reshape(devices, capacity, NBIN),
            ("sky", "zb"),
            split_axis=0,
            concat_axis=0,
            tiled=True,
        ),
        lax.all_to_all(
            pixel_send.reshape(devices, capacity),
            ("sky", "zb"),
            split_axis=0,
            concat_axis=0,
            tiled=True,
        ),
    )
    pdf_rows = received.reshape(slot_total, NBIN)
    slot_labels = labels.reshape(slot_total)
    pdf_split = pdf_rows.reshape(slot_total, zb_size, bin_share)
    owner_count = lax.axis_size(("sky", "zb")) * PIX_DEV // PIX_DEV
    owners = jnp.arange(owner_count, dtype=jnp.int32)
    pixel_index = (owners // zb_size)[:, None] * PIX_DEV + jnp.arange(PIX_DEV, dtype=jnp.int32)[
        None, :
    ]
    selector = (pixel_index[:, :, None] == slot_labels[None, None, :]).astype(jnp.bfloat16)
    chooser = (jnp.arange(zb_size, dtype=jnp.int32)[None, :] == (owners % zb_size)[:, None]).astype(
        jnp.bfloat16
    )
    chosen = jnp.einsum(
        "mz,szb->msb", chooser, pdf_split, preferred_element_type=jnp.float32
    ).astype(jnp.bfloat16)
    summed = jnp.einsum("mps,msb->mpb", selector, chosen, preferred_element_type=jnp.float32)
    nz_map = lax.psum_scatter(
        summed.reshape(lax.axis_size(("sky", "zb")) * PIX_DEV, bin_share),
        ("sky", "zb"),
        scatter_dimension=0,
        tiled=True,
    )
    return (pdf_rows, nz_map)


def solution(mesh):
    in_specs = (
        P(("sky", "zb"), None),
        P(("sky", "zb")),
        P(("sky", "zb"), None),
        P(("sky", "zb")),
        P(),
        P(),
        P(),
        P(),
        P(),
    )
    out_specs = (P(("sky", "zb"), None), P("sky", "zb"))
    return jax.shard_map(local, mesh=mesh, in_specs=in_specs, out_specs=out_specs, check_vma=False)
```

profile of v0, /device:TPU:1, one launch (start us, length us, event | category | flops | bytes accessed | tf_op | source)
XLA Modules:
  0.0 797.1 jit_solution(5181868362397834204)
XLA Ops:
  7.2 0.0 copy-start
  7.2 1.0 convert_reduce_fusion
  8.2 0.7 compare_select_fusion.1
  9.5 0.7 broadcast_select_fusion
  10.2 2.4 scatter_custom_fusion.1
  12.7 0.7 all_to_all.10
  13.4 11.5 %all-to-all-start.1 = ((s32[128,1,8]{2,1,0:T(1,128)}), s32[128,1,8]{2,1,0:T(1,128)S(1)}, u32[]{:S(2)}, u32[]{:S(2)}) async-start(s32[128,1,8]{2,1,0:T(1,128)} %bitcast.8), calls=%async_computation.1 | async-start | bytes 131072 | tf_op jit(solution)/shard_map/all_to_all | solution.py:87
  24.9 8.0 copy.35
  32.9 10.7 %reshape.92 = bf16[512,32,32,5]{0,3,2,1:T(8,128)(2,1)} reshape(bf16[512,5120]{0,1:T(8,128)(2,1)} %copy.35) | data formatting | bytes 10485760 | tf_op jit(solution)/shard_map/reshape | solution.py:50
  43.5 0.1 shard_map.108
  43.7 12.2 %maximum_convert_fusion = bf16[512,16,16,64]{0,3,2,1:T(8,128)(2,1)} fusion(bf16[512,32,32,5]{0,3,2,1:T(8,128)(2,1)} %reshape.92, bf16[3,3,5,64]{3,1,2,0:T(4,128)(2,1)S(1)} %copy-done.3), kind=kOutput, calls=%fused_computation.2 | convolution fusion | flops 740622336 | bytes 22025856 | tf_op jit(solution)/shard_map/conv_general_dilated | solution.py:22
  55.8 15.8 %maximum_convert_fusion.2 = bf16[512,4,4,2,128]{0,4,3,2,1:T(8,128)(2,1)} fusion(bf16[512,16,16,2,32]{0,4,3,2,1:T(8,128)(2,1)} %bitcast.32, bf16[3,3,32,2,64]{4,3,2,1,0:T(2,128)(2,1)S(1)} %shard_map.108, bf16[3,3,64,256]{3,2,1,0:T(8,128)(2,1)S(1)} %copy-done), kind=kOutput, calls=%fused_computation.14 | convolution fusion | flops 4261412864 | bytes 21340160 | tf_op jit(solution)/shard_map/conv_general_dilated | solution.py:22
  71.6 6.0 fusion.8
  77.6 0.1 fusion.31
  77.7 3.9 add_multiply_fusion
  81.6 6.8 fusion.3
  88.4 0.3 copy.43
  88.7 3.7 scatter_custom_fusion
  92.5 9.8 %all-to-all-start = ((bf16[128,8,512]{2,1,0:T(8,128)(2,1)}), bf16[128,8,512]{2,1,0:T(8,128)(2,1)S(1)}, u32[]{:S(2)}, u32[]{:S(2)}) async-start(bf16[128,8,512]{2,1,0:T(8,128)(2,1)} %bitcast.6), calls=%async_computation | async-start | bytes 2097152 | tf_op jit(solution)/shard_map/all_to_all | solution.py:80
  102.2 0.0 reduce-scatter.2.cloned.1.call-start
  102.3 0.1 iota_add_fusion
  102.4 0.5 broadcast.114
  102.9 0.8 reduce.3
  103.7 0.1 eq.50
  103.8 17.8 %all-to-all-done = bf16[128,8,512]{2,1,0:T(8,128)(2,1)S(1)} async-done(((bf16[128,8,512]{2,1,0:T(8,128)(2,1)}), bf16[128,8,512]{2,1,0:T(8,128)(2,1)S(1)}, u32[]{:S(2)}, u32[]{:S(2)}) %all-to-all-start) | async-done | bytes 1048608 | tf_op jit(solution)/shard_map/all_to_all | solution.py:80
  121.6 1.1 reshape_reshape.3
  122.7 3.3 copy.41
  126.0 11.5 %convolution_convert_fusion = bf16[128,1024,64]{1,0,2:T(8,128)(2,1)} fusion(bf16[1024,8,64]{0,1,2:T(8,128)(2,1)} %copy.41, s32[128]{0:T(128)S(1)} %and_select_fusion), kind=kOutput, calls=%fused_computation.13 | convolution fusion | flops 142607360 | bytes 17826304 | tf_op jit(solution)/shard_map/mz,szb->msb/dot_general | solution.py:107
  137.5 19.8 %fusion = f32[128,64,64]{2,1,0:T(8,128)} fusion(bf16[128,1024,64]{1,0,2:T(8,128)(2,1)} %convolution_convert_fusion, s32[1024]{0:T(1024)S(1)} %eq.50, s32[128,64]{1,0:T(8,128)S(1)} %iota_add_fusion), kind=kOutput, calls=%fused_computation.3 | convolution fusion | flops 1082130432 | bytes 18911232 | tf_op jit(solution)/shard_map/mps,msb->mpb/dot_general | solution.py:110
  157.3 0.0 reduce-scatter.2.cloned.1.call-update
  157.3 632.0 %reduce-scatter.2.cloned.1.call-done = f32[64,64]{1,0:T(8,128)} async-done(((f32[8192,64]{1,0:T(8,128)}), f32[64,64]{1,0:T(8,128)}) %reduce-scatter.2.cloned.1.call-update) | async-done | bytes 16400 | tf_op jit(solution)/shard_map/reduce_scatter | solution.py:111
  789.3 1.0 copy.58
  (15 shorter events, 0.1 us)
Async XLA Ops:
  7.2 48.7 %copy-start = (bf16[3,3,64,256]{3,2,1,0:T(8,128)(2,1)S(1)}, bf16[3,3,64,256]{3,2,1,0:T(8,128)(2,1)}, u32[]{:S(2)}) copy-start(bf16[3,3,64,256]{3,2,1,0:T(8,128)(2,1)} %param.15) | copy-start | bytes 884740
  7.2 36.4 %copy-start.2 = (bf16[3,3,32,128]{3,2,1,0:T(8,128)(2,1)S(1)}, bf16[3,3,32,128]{3,2,1,0:T(8,128)(2,1)}, u32[]{:S(2)}) copy-start(bf16[3,3,32,128]{3,2,1,0:T(8,128)(2,1)} %param.14) | copy-start | bytes 221188
  7.2 36.5 %copy-start.3 = (bf16[3,3,5,64]{3,1,2,0:T(4,128)(2,1)S(1)}, bf16[3,3,5,64]{3,1,2,0:T(4,128)(2,1)}, u32[]{:S(2)}) copy-start(bf16[3,3,5,64]{3,1,2,0:T(4,128)(2,1)} %param.13) | copy-start | bytes 17284
  13.4 79.1 %all-to-all-start.1 = ((s32[128,1,8]{2,1,0:T(1,128)}), s32[128,1,8]{2,1,0:T(1,128)S(1)}, u32[]{:S(2)}, u32[]{:S(2)}) async-start(s32[128,1,8]{2,1,0:T(1,128)} %bitcast.8), calls=%async_computation.1 | async-start | bytes 131072 | tf_op jit(solution)/shard_map/all_to_all | solution.py:87
  55.8 15.8 %copy-start.4 = (bf16[512,48]{0,1:T(8,128)(2,1)S(1)}, bf16[512,48]{0,1:T(8,128)(2,1)}, u32[]{:S(2)}) copy-start(bf16[512,48]{0,1:T(8,128)(2,1)} %param.17) | copy-start | bytes 147460
  92.5 29.1 %all-to-all-start = ((bf16[128,8,512]{2,1,0:T(8,128)(2,1)}), bf16[128,8,512]{2,1,0:T(8,128)(2,1)S(1)}, u32[]{:S(2)}, u32[]{:S(2)}) async-start(bf16[128,8,512]{2,1,0:T(8,128)(2,1)} %bitcast.6), calls=%async_computation | async-start | bytes 2097152 | tf_op jit(solution)/shard_map/all_to_all | solution.py:80
  102.2 687.1 %reduce-scatter.2.cloned.1.call-start = ((), (), s32[]{:S(2)}) async-start(), calls=%async_computation.3 | async-start | bytes 4227072 | tf_op jit(solution)/shard_map/reduce_scatter | solution.py:111
  126.0 664.3 %copy-start.1 = (bf16[3,3,64,256]{3,2,1,0:T(8,128)(2,1)S(1)}, bf16[3,3,64,256]{3,2,1,0:T(8,128)(2,1)}, u32[]{:S(2)}) copy-start(bf16[3,3,64,256]{3,2,1,0:T(8,128)(2,1)} %param.15) | copy-start | bytes 884740
Sparse Core Ops, SparseCore 0:
  157.5 631.8 reduce-scatter.1
where the time goes:
time: 804 us; the launch traced here: 797 us
  waiting for transfers between devices  650 us (81%)
  matrix products  65.3 us (8%)
  local copies, waits for them, and re-layouts  28.2 us (4%)
  starting transfers between devices  21.3 us (3%)
  other arithmetic  17.8 us (2%)
  between operations  14.8 us (2%)
    reduce_scatter x1, waiting for transfers between devices, local(): lax.psum_scatter(summed.reshape(lax.axis_size(('sky', 'zb')) * PIX_DEV, b...  632 us
    conv_general_dilated x2, matrix products, convolve(): lax.conv_general_dilated(images, kernel, (2, 2), ((1, 1), (1, 1)), dimens...  27.9 us
    dot_general x1, matrix products, local(): jnp.einsum('mps,msb->mpb', selector, chosen, preferred_element_type=jnp.f...  19.8 us
    all_to_all x1, waiting for transfers between devices, local(): lax.all_to_all(pdf_send.reshape(devices, capacity, NBIN), ('sky', 'zb'),...  17.8 us
  transfers between devices with their start and end apart: 3, of which 2 were waited for; matrix products, arithmetic and copies ran while one was open for 9% of the time, Pallas kernels for 0%

commit v1 on v0

--- a/solution.py
+++ b/solution.py
@@ -5,12 +5,12 @@
 from jax import lax
 from jax.sharding import PartitionSpec as P
 
-PIX_DEV = 64
 NBIN = 512
 NCOMP = 16
 BANDS = 5
 STAMP = 32
 GROUPS = 2
+NPIX = 1024
 
 
 Z_TOP = 3.0
@@ -61,60 +61,47 @@
 def local(stamps, counts, dest, pixel_ids, conv1_w, conv2_w, conv3_w, dense_w, head_w):
     devices = lax.axis_size(("sky", "zb"))
     zb_size = lax.axis_size("zb")
+    sky_size = lax.axis_size("sky")
     row_total = stamps.shape[0]
     capacity = max(2, 2 * row_total // devices)
     slot_total = devices * capacity
     bin_share = NBIN // zb_size
+    pix_share = NPIX // sky_size
     row_order = jnp.arange(row_total, dtype=jnp.int32)
     is_valid = row_order < counts[0]
     target = dest[:, 0]
     before = (target[:, None] == target[None, :]) & (row_order[None, :] < row_order[:, None])
     slot_rank = jnp.sum(before.astype(jnp.int32), axis=1)
     position = target * capacity + slot_rank
-    tagged = jnp.where(is_valid, pixel_ids, -1)
-    pixel_send = jnp.full((slot_total,), -1, jnp.int32).at[position].set(tagged)
     density = network(stamps, conv1_w, conv2_w, conv3_w, dense_w, head_w)
     density = jnp.where(is_valid[:, None], density, 0.0).astype(jnp.bfloat16)
-    pdf_send = jnp.zeros((slot_total, NBIN), jnp.bfloat16).at[position].set(density)
-    received, labels = (
-        lax.all_to_all(
-            pdf_send.reshape(devices, capacity, NBIN),
-            ("sky", "zb"),
-            split_axis=0,
-            concat_axis=0,
-            tiled=True,
-        ),
-        lax.all_to_all(
-            pixel_send.reshape(devices, capacity),
-            ("sky", "zb"),
-            split_axis=0,
-            concat_axis=0,
-            tiled=True,
-        ),
-    )
-    pdf_rows = received.reshape(slot_total, NBIN)
-    slot_labels = labels.reshape(slot_total)
-    pdf_split = pdf_rows.reshape(slot_total, zb_size, bin_share)
-    owner_count = lax.axis_size(("sky", "zb")) * PIX_DEV // PIX_DEV
-    owners = jnp.arange(owner_count, dtype=jnp.int32)
-    pixel_index = (owners // zb_size)[:, None] * PIX_DEV + jnp.arange(PIX_DEV, dtype=jnp.int32)[
-        None, :
-    ]
-    selector = (pixel_index[:, :, None] == slot_labels[None, None, :]).astype(jnp.bfloat16)
-    chooser = (jnp.arange(zb_size, dtype=jnp.int32)[None, :] == (owners % zb_size)[:, None]).astype(
+    place = (jnp.arange(slot_total, dtype=jnp.int32)[:, None] == position[None, :]).astype(
         jnp.bfloat16
     )
-    chosen = jnp.einsum(
-        "mz,szb->msb", chooser, pdf_split, preferred_element_type=jnp.float32
+    pdf_send = jnp.dot(place, density, preferred_element_type=jnp.float32).astype(jnp.bfloat16)
+    pdf_send = pdf_send.reshape(devices, capacity, NBIN)
+    pair = (jnp.arange(NPIX // 2, dtype=jnp.int32)[:, None] == (pixel_ids // 2)[None, :]).astype(
+        jnp.bfloat16
+    )
+    odd = (pixel_ids % 2 == 1)[:, None, None]
+    split = density.reshape(row_total, zb_size, bin_share)
+    zero = jnp.zeros_like(split)
+    both = jnp.stack([jnp.where(odd, zero, split), jnp.where(odd, split, zero)], axis=2)
+    partial = jnp.dot(
+        pair, both.reshape(row_total, 2 * NBIN), preferred_element_type=jnp.float32
     ).astype(jnp.bfloat16)
-    summed = jnp.einsum("mps,msb->mpb", selector, chosen, preferred_element_type=jnp.float32)
-    nz_map = lax.psum_scatter(
-        summed.reshape(lax.axis_size(("sky", "zb")) * PIX_DEV, bin_share),
+    map_send = partial.reshape(sky_size, pix_share // 2, zb_size, 2 * bin_share)
+    map_send = map_send.transpose(0, 2, 1, 3).reshape(devices, capacity, NBIN)
+    received = lax.all_to_all(
+        jnp.concatenate([pdf_send, map_send], axis=1),
         ("sky", "zb"),
-        scatter_dimension=0,
+        split_axis=0,
+        concat_axis=0,
         tiled=True,
     )
-    return (pdf_rows, nz_map)
+    pdf_rows = received[:, :capacity].reshape(slot_total, NBIN)
+    nz_map = jnp.sum(received[:, capacity:].astype(jnp.float32), axis=0)
+    return (pdf_rows, nz_map.reshape(pix_share, bin_share))
 
 
 def solution(mesh):

time: 804 us -> 114 us (0.14)
  waiting for transfers between devices: 650 us -> 0 us
  blocking collectives: 0 us -> 41.8 us
  matrix products: 65.3 us -> 35.5 us
  starting transfers between devices: 21.3 us -> 0 us
  between operations: 14.8 us -> 1.47 us
    reduce_scatter x1 -> x0, waiting for transfers between devices: 632 us -> none  [local(): lax.psum_scatter(summed.reshape(lax.axis_size(('sky', 'zb')) * PIX_DEV, b...]
    all_to_all x0 -> x1, blocking collectives: none -> 41.8 us  [local(): lax.all_to_all(jnp.concatenate([pdf_send, map_send], axis=1), ('sky', 'zb...]
    dot_general x2, matrix products: 31.3 us -> 1.54 us  [the longest x1 0.79 us: local(): jnp.dot(place, density, preferred_element_type=jnp.float32)]
    all_to_all x2 -> x0, starting transfers between devices: 21.3 us -> none  [the longest x1 11.5 us: local(): lax.all_to_all(pixel_send.reshape(devices, capacity), ('sky', 'zb'), spli...]
    all_to_all x2 -> x0, waiting for transfers between devices: 17.8 us -> none  [the longest x1 17.8 us: local(): lax.all_to_all(pdf_send.reshape(devices, capacity, NBIN), ('sky', 'zb'),...]
  transfers between devices with their start and end apart: 3 -> 0, of which waited for: 2 -> 0; matrix products, arithmetic and copies ran while one was open for 9% -> 0% of each run, Pallas kernels for 0% -> 0%
where the time goes in v1:
time: 114 us; the launch traced here: 113 us
  blocking collectives  41.8 us (37%)
  matrix products  35.5 us (31%)
  local copies, waits for them, and re-layouts  22.1 us (19%)
  other arithmetic  12.2 us (11%)
  between operations  1.47 us (1%)
    all_to_all x1, blocking collectives, local(): lax.all_to_all(jnp.concatenate([pdf_send, map_send], axis=1), ('sky', 'zb...  41.8 us
    conv_general_dilated x2, matrix products, convolve(): lax.conv_general_dilated(images, kernel, (2, 2), ((1, 1), (1, 1)), dimens...  27.9 us
    reshape x1, local copies, waits for them, and re-layouts, network(): stamp_grid = images.reshape(amount, STAMP, STAMP, BANDS)  10.7 us
    unnamed x17, local copies, waits for them, and re-layouts  8.52 us
    reduce_sum x1, other arithmetic, mixture(): return jnp.sum(shares[:, :, None] * masses, axis=1)  7.13 us
    dot_general x1, matrix products, network(): head_out = jnp.dot(hidden, head_w, preferred_element_type=jnp.float32)  6 us
    mul x1, other arithmetic, mixture(): cumulative = 0.5 * (1.0 + lax.erf(scaled))  3.86 us

profile of v1, /device:TPU:1, one launch (start us, length us, event | category | flops | bytes accessed | tf_op | source)
XLA Modules:
  0.0 113.1 jit_solution(3891764962589951823)
XLA Ops:
  0.6 0.0 copy-start
  0.7 8.0 %copy.28 = bf16[512,5120]{0,1:T(8,128)(2,1)} copy(bf16[512,5120]{1,0:T(8,128)(2,1)} %param.9) | data formatting | bytes 10485760 | tf_op args[0]
  8.7 10.7 %reshape.90 = bf16[512,32,32,5]{0,3,2,1:T(8,128)(2,1)} reshape(bf16[512,5120]{0,1:T(8,128)(2,1)} %copy.28) | data formatting | bytes 10485760 | tf_op jit(solution)/shard_map/reshape | solution.py:50
  19.3 0.0 copy-done.2
  19.4 0.1 shard_map.108
  19.5 0.0 copy-done.3
  19.5 12.2 %maximum_convert_fusion = bf16[512,16,16,64]{0,3,2,1:T(8,128)(2,1)} fusion(bf16[512,32,32,5]{0,3,2,1:T(8,128)(2,1)} %reshape.90, bf16[3,3,5,64]{3,1,2,0:T(4,128)(2,1)S(1)} %copy-done.3), kind=kOutput, calls=%fused_computation | convolution fusion | flops 740622336 | bytes 22025856 | tf_op jit(solution)/shard_map/conv_general_dilated | solution.py:22
  31.6 0.0 copy-done
  31.6 15.8 %maximum_convert_fusion.2 = bf16[512,4,4,2,128]{0,4,3,2,1:T(8,128)(2,1)} fusion(bf16[512,16,16,2,32]{0,4,3,2,1:T(8,128)(2,1)} %bitcast.38, bf16[3,3,32,2,64]{4,3,2,1,0:T(2,128)(2,1)S(1)} %shard_map.108, bf16[3,3,64,256]{3,2,1,0:T(8,128)(2,1)S(1)} %copy-done), kind=kOutput, calls=%fused_computation.6 | convolution fusion | flops 4261412864 | bytes 21340160 | tf_op jit(solution)/shard_map/conv_general_dilated | solution.py:22
  47.4 0.0 copy-done.6
  47.4 6.0 %fusion.7 = f32[512,48]{0,1:T(8,128)S(1)} fusion(bf16[512,48]{0,1:T(8,128)(2,1)S(1)} %copy-done.6, bf16[512,4096]{0,1:T(8,128)(2,1)} %bitcast.44, bf16[4096,512]{1,0:T(8,128)(2,1)} %param.16), kind=kOutput, calls=%fused_computation.17 | convolution fusion | flops 2173173760 | bytes 8536064 | tf_op jit(solution)/shard_map/dot_general | solution.py:57
  53.4 0.1 fusion.30
  54.2 3.9 %add_multiply_fusion = f32[512,16,513]{0,1,2:T(8,128)S(1)} fusion(f32[512,16]{0,1:T(8,128)S(1)} %get-tuple-element.5, f32[512,16]{0,1:T(8,128)S(1)} %get-tuple-element.6, f32[513]{0:T(1024)S(1)} %iota_multiply_fusion), kind=kLoop, calls=%fused_computation.1 | loop fusion | flops 16809984 | bytes 16877572 | tf_op jit(solution)/shard_map/mul | solution.py:43
  58.1 7.1 %fusion.1 = bf16[512,512]{0,1:T(8,128)(2,1)S(1)} fusion(f32[512,16,513]{0,1,2:T(8,128)S(1)} %add_multiply_fusion, f32[512,16]{0,1:T(8,128)S(1)} %get-tuple-element.4), kind=kLoop, calls=%fused_computation.4 | loop fusion | flops 12320768 | bytes 34111488 | tf_op jit(solution)/shard_map/reduce_sum | solution.py:45
  65.2 0.2 copy.36
  65.5 0.0 copy-start.4
  65.5 0.2 broadcast_select_fusion.1
  65.7 0.1 pad_maximum_fusion.1
  65.8 0.1 copy.34
  65.9 0.7 fusion.5
  66.6 0.3 copy.38
  66.9 0.1 bitcast_bitcast_fusion
  67.0 0.0 copy-start.1
  67.0 0.2 copy.35
  67.3 0.7 reshape.94
  67.9 0.2 convert_reduce_fusion.1
  68.2 0.8 fusion.4
  69.0 0.3 pad_maximum_fusion
  69.3 41.8 %all_to_all.5 = bf16[128,16,512]{2,1,0:T(8,128)(2,1)S(1)} all-to-all(bf16[128,16,512]{2,1,0:T(8,128)(2,1)S(1)} %pad_maximum_fusion), channel_id=1, replica_groups=mesh['sky'=16,'zb'=8] {'sky','zb'}, dimensions={0} | all-to-all | bytes 4194304 | tf_op jit(solution)/shard_map/all_to_all | solution.py:95
  111.1 0.2 convert_reduce_fusion
  111.3 0.7 reshape.96
  112.0 1.1 slice_bitcast_fusion
  (12 shorter events, 0.1 us)
Async XLA Ops:
  0.6 31.0 %copy-start = (bf16[3,3,64,256]{3,2,1,0:T(8,128)(2,1)S(1)}, bf16[3,3,64,256]{3,2,1,0:T(8,128)(2,1)}, u32[]{:S(2)}) copy-start(bf16[3,3,64,256]{3,2,1,0:T(8,128)(2,1)} %param.15) | copy-start | bytes 884740
  8.7 10.7 %copy-start.2 = (bf16[3,3,32,128]{3,2,1,0:T(8,128)(2,1)S(1)}, bf16[3,3,32,128]{3,2,1,0:T(8,128)(2,1)}, u32[]{:S(2)}) copy-start(bf16[3,3,32,128]{3,2,1,0:T(8,128)(2,1)} %param.14) | copy-start | bytes 221188
  8.7 10.8 %copy-start.3 = (bf16[3,3,5,64]{3,1,2,0:T(4,128)(2,1)S(1)}, bf16[3,3,5,64]{3,1,2,0:T(4,128)(2,1)}, u32[]{:S(2)}) copy-start(bf16[3,3,5,64]{3,1,2,0:T(4,128)(2,1)} %param.13) | copy-start | bytes 17284
  31.6 15.8 %copy-start.6 = (bf16[512,48]{0,1:T(8,128)(2,1)S(1)}, bf16[512,48]{0,1:T(8,128)(2,1)}, u32[]{:S(2)}) copy-start(bf16[512,48]{0,1:T(8,128)(2,1)} %param.17) | copy-start | bytes 147460
  47.4 6.8 %copy-start.5 = (s32[512]{0:T(512)S(1)}, s32[512]{0:T(512)}, u32[]{:S(2)}) copy-start(s32[512]{0:T(512)} %param.12) | copy-start | bytes 6148
  65.5 2.5 %copy-start.4 = (s32[512,1]{0,1:T(1,128)S(1)}, s32[512,1]{0,1:T(1,128)}, u32[]{:S(2)}) copy-start(s32[512,1]{0,1:T(1,128)} %param.11) | copy-start | bytes 6148
  67.0 46.1 %copy-start.1 = (bf16[3,3,64,256]{3,2,1,0:T(8,128)(2,1)S(1)}, bf16[3,3,64,256]{3,2,1,0:T(8,128)(2,1)}, u32[]{:S(2)}) copy-start(bf16[3,3,64,256]{3,2,1,0:T(8,128)(2,1)} %param.15) | copy-start | bytes 884740

commit v2 on v1

v2 whole, which is shorter than its diff:
```python
import functools
import math

import jax
import jax.numpy as jnp
from jax import lax
from jax.experimental import pallas as pl
from jax.experimental.pallas import tpu as pltpu
from jax.sharding import PartitionSpec as P

ROWS = 512
NBIN = 512
NCOMP = 16
BANDS = 5
STAMP = 32
PIXELS = STAMP * STAMP * BANDS
NPIX = 1024
C1 = 64
C2 = 128
C3 = 256
HIDDEN = 512
CAP = 8
DEVICES = 128
SKY = 16
ZB = 8
PIX_DEV = NPIX // SKY
BIN_DEV = NBIN // ZB
MAP_ROWS = PIX_DEV * BIN_DEV // 128
BLOCK = MAP_ROWS + CAP
FRONT = 256
PITCH = 1024
EDGE_ROWS = 520

Z_TOP = 3.0
SPREAD_LOW = 0.05
SPREAD_RANGE = 0.25

F32 = jnp.float32
BF16 = jnp.bfloat16


def iota(shape, dim):
    return lax.broadcasted_iota(jnp.int32, shape, dim)


def relu16(values):
    return jnp.maximum(values, 0.0).astype(BF16)


def dot(left, right):
    return jnp.dot(left, right, preferred_element_type=F32)


def dot_nt(left, right):
    return lax.dot_general(left, right, (((1,), (1,)), ((), ())), preferred_element_type=F32)


def spread_first(w1_ref, w1_s, t1_s):
    w1_s[...] = jnp.zeros_like(w1_s)
    for kh in range(3):
        for kw in range(3):
            w1_s[kw, pl.ds(kh * BANDS, BANDS), :] = w1_ref[kh, kw].astype(F32)
    chan, lane = iota((C1, 512), 0), iota((C1, 512), 1)
    repeat = (chan == (lane >= 256) * 32 + (lane & 31)).astype(F32).astype(BF16)

    def row_parts(shape):
        k = iota(shape, 0)
        kh = (k >= 85).astype(jnp.int32) + (k >= 170).astype(jnp.int32)
        rem = k - 85 * kh
        col = (rem * 205) >> 10
        return k, kh, col, rem - 5 * col

    k, kh, col, band = row_parts((256, 16))
    pick = ((iota((256, 16), 1) == kh * BANDS + band) & (k < 255)).astype(F32).astype(BF16)
    k, kh, col, band = row_parts((256, 512))
    tap = col - 2 * ((iota((256, 512), 1) & 255) >> 5)
    total = jnp.zeros((256, 512), F32)
    for kw in range(3):
        lanes = dot(w1_s[kw].astype(BF16), repeat).astype(BF16)
        total = jnp.where(tap == kw, dot(pick, lanes), total)
    t1_s[1] = total.astype(BF16)
    t1_s[0] = jnp.where(col == 0, 0.0, total).astype(BF16)


def spread_second(w2_ref, w2a_s, w2b_s):
    w2a_s[...] = jnp.zeros_like(w2a_s)
    w2b_s[...] = jnp.zeros_like(w2b_s)
    low = iota((32, 128), 1) < 64
    zero = jnp.zeros((32, 128), F32)
    for kh in range(3):
        plain = [w2_ref[kh, kw].astype(F32) for kw in range(3)]
        swapped = [pltpu.roll(tap, 64, 1) for tap in plain]
        for g in range(2):
            lo = plain if g == 0 else swapped
            hi = swapped if g == 0 else plain
            for d in range(-1, 4):
                first = lo[d + 1] if d + 1 <= 2 else zero
                second = hi[d - 1] if d >= 1 else zero
                tile = jnp.where(low, first, second).astype(BF16)
                for q in range(2):
                    c = d + 4 * q
                    if -1 <= c <= 7:
                        at = kh * 384 + 128 + 32 * c
                        w2b_s[g, at : at + 32, 128 * q : 128 * q + 128] = tile
                    if 0 <= c <= 7:
                        at = kh * 256 + 32 * c
                        w2a_s[g, at : at + 32, 128 * q : 128 * q + 128] = tile


def spread_third(w3_ref, w3a_s, w3b_s):
    w3a_s[...] = jnp.zeros_like(w3a_s)
    w3b_s[...] = jnp.zeros_like(w3b_s)
    for kh in range(3):
        for kw in range(3):
            for g in range(2):
                tap = w3_ref[kh, kw, :, g * 128 : g * 128 + 128]
                for oc in range(2):
                    c = kw + 2 * oc - 1
                    at = kh * 384 + 128 + 64 * c
                    w3b_s[g, at : at + 64, 128 * oc : 128 * oc + 128] = tap
                    if c >= 0:
                        at = kh * 256 + 64 * c
                        w3a_s[g, at : at + 64, 128 * oc : 128 * oc + 128] = tap


def grouped(source, row, wa_s, wb_s, store):
    for g in range(2):
        for half in range(2):
            width = 384 if half else 256
            parts = []
            for kh in range(3):
                at = pl.multiple_of((2 * row + kh) * PITCH, PITCH) + (g * 512 + half * 128)
                parts.append(source[:, pl.ds(pl.multiple_of(at, 128), width)])
            weights = wb_s[g] if half else wa_s[g]
            store(g, half, relu16(dot(jnp.concatenate(parts, axis=1), weights)))


def coefficients(logits, mids, widths, axis, live):
    share = jnp.maximum(logits, 0.0) + jnp.log1p(jnp.exp(-jnp.abs(logits))) + 0.1
    return share, Z_TOP * jax.nn.sigmoid(mids), 1.0 / (
        (SPREAD_LOW + SPREAD_RANGE * jax.nn.sigmoid(widths)) * math.sqrt(2.0)
    )


def owner_kernel(
    counts_ref, dest_ref, pixel_ref, x_hbm, w1_ref, w2_ref, w3_ref, wd_hbm, wh_ref,
    send_ref,
    x_s, wd_s, l1_s, l2_s, l3_s, w1_s, t1_s, w2a_s, w2b_s, w3a_s, w3b_s, coef_s, cdf_s, den_s,
    sems,
):
    x_copy = pltpu.make_async_copy(x_hbm, x_s.at[:, pl.ds(FRONT, PIXELS)], sems.at[0])
    x_copy.start()
    d_copy = pltpu.make_async_copy(wd_hbm, wd_s, sems.at[1])
    d_copy.start()
    x_s[:, 0:FRONT] = jnp.zeros((ROWS, FRONT), BF16)
    l1_s[:, 0:PITCH] = jnp.zeros((ROWS, PITCH), BF16)
    l2_s[:, 0:PITCH] = jnp.zeros((ROWS, PITCH), BF16)
    spread_first(w1_ref, w1_s, t1_s)
    spread_second(w2_ref, w2a_s, w2b_s)
    spread_third(w3_ref, w3a_s, w3b_s)
    x_copy.wait()

    def first(t, carry):
        x = x_s[:, pl.ds(pl.multiple_of(t * 640, 128), 896)]
        for odd in range(2):
            for half in range(2):
                start = 91 + 320 * odd + 80 * half
                window = jnp.concatenate(
                    [x[:, start + 160 * kh : start + 160 * kh + 85] for kh in range(3)]
                    + [jnp.zeros((ROWS, 1), BF16)],
                    axis=1,
                )
                out = relu16(dot(window, t1_s[half]))
                at = pl.multiple_of((2 * t + odd + 1) * PITCH, PITCH)
                for g in range(2):
                    l1_s[:, pl.ds(pl.multiple_of(at + (g * 512 + half * 256), 128), 256)] = out[
                        :, g * 256 : g * 256 + 256
                    ]
        return carry

    lax.fori_loop(0, STAMP // 4, first, 0)

    def second(r, carry):
        def store(g, half, out):
            at = pl.multiple_of((r + 1) * PITCH, PITCH) + (g * 512 + half * 256)
            l2_s[:, pl.ds(pl.multiple_of(at, 128), 256)] = out

        grouped(l1_s, r, w2a_s, w2b_s, store)
        return carry

    lax.fori_loop(0, STAMP // 4, second, 0)

    def third(r, carry):
        def store(g, half, out):
            for oc in range(2):
                at = pl.multiple_of(r * 1024, 1024) + ((2 * half + oc) * 256 + g * 128)
                l3_s[:, pl.ds(pl.multiple_of(at, 128), 128)] = out[:, oc * 128 : oc * 128 + 128]

        grouped(l2_s, r, w3a_s, w3b_s, store)
        return carry

    lax.fori_loop(0, STAMP // 8, third, 0)
    d_copy.wait()
    hidden = relu16(dot(l3_s[...], wd_s[...]))
    wh = wh_ref[...]
    head = dot(hidden, jnp.concatenate([wh, wh, jnp.zeros((HIDDEN, 32), BF16)], axis=1))

    count = counts_ref[0]
    high = head.astype(BF16).astype(F32)
    lane = iota((ROWS, 128), 1)
    alive = (iota((ROWS, 128), 0) < count).astype(F32)
    params = jnp.where(lane < 48, high, jnp.where(lane < 96, head - high, alive)).astype(BF16)
    dest = dest_ref[...]
    named = iota((DEVICES, ROWS), 0) == dest
    named16 = named.astype(F32).astype(BF16)
    earlier = (iota((ROWS, ROWS), 0) < iota((ROWS, ROWS), 1)).astype(F32).astype(BF16)
    rank = jnp.sum(jnp.where(named, dot(named16, earlier), 0.0), axis=0, keepdims=True)
    position = dest * CAP + rank.astype(jnp.int32)
    place = (iota((DEVICES * CAP, ROWS), 0) == position).astype(F32).astype(BF16)
    slots = dot(place, params).reshape(DEVICES, CAP, 128)
    send_ref[:, MAP_ROWS:BLOCK, :] = slots.astype(BF16)

    turned = head.T
    share, centre, inverse = coefficients(
        turned[0:16], turned[16:32], turned[32:48], 0, None
    )
    live = (iota((1, ROWS), 1) < count).astype(F32)
    coef_s[0] = share * (0.5 * live / jnp.sum(share, axis=0, keepdims=True))
    coef_s[1] = centre
    coef_s[2] = inverse
    blocks, depth = 5, EDGE_ROWS // 5

    def mix(step, carry):
        block, tile = step // 4, step % 4
        lanes = pl.ds(pl.multiple_of(tile * 128, 128), 128)
        rows = pl.multiple_of(block * depth, 8)
        edge = (iota((depth, 128), 0) + rows).astype(F32) * Z_TOP / NBIN
        total = jnp.zeros((depth, 128), F32)
        for k in range(NCOMP):
            scaled = (edge - coef_s[1, k : k + 1, lanes]) * coef_s[2, k : k + 1, lanes]
            total = total + coef_s[0, k : k + 1, lanes] * lax.erf(scaled)
        cdf_s[pl.ds(rows, depth), lanes] = total
        return carry

    lax.fori_loop(0, blocks * 4, mix, 0)
    density = (cdf_s[1 : NBIN + 1, :] - cdf_s[0:NBIN, :]).astype(BF16).astype(F32)

    pixel = pixel_ref[...]
    odd = (pixel & 1).astype(F32)
    for j in range(ZB):
        part = density[j * BIN_DEV : (j + 1) * BIN_DEV]
        den_s[j * 128 : j * 128 + 64, :] = (part * (1.0 - odd)).astype(BF16)
        den_s[j * 128 + 64 : j * 128 + 128, :] = (part * odd).astype(BF16)
    pair = (iota((NPIX // 2, ROWS), 0) == (pixel >> 1)).astype(F32).astype(BF16)
    for q in range(ZB // 2):
        maps = dot_nt(pair, den_s[q * 256 : q * 256 + 256, :]).astype(BF16)
        for s in range(SKY):
            for j in range(2):
                send_ref[s * ZB + 2 * q + j, 0:MAP_ROWS, :] = maps[
                    s * MAP_ROWS : (s + 1) * MAP_ROWS, j * 128 : j * 128 + 128
                ]


def owner(stamps, counts, dest, pixel_ids, conv1_w, conv2_w, conv3_w, dense_w, head_w):
    vmem = pl.BlockSpec(memory_space=pltpu.VMEM)
    hbm = pl.BlockSpec(memory_space=pl.ANY)
    return pl.pallas_call(
        owner_kernel,
        out_shape=jax.ShapeDtypeStruct((DEVICES, BLOCK, 128), BF16),
        in_specs=[pl.BlockSpec(memory_space=pltpu.SMEM), vmem, vmem, hbm, vmem, vmem, vmem, hbm, vmem],
        out_specs=vmem,
        scratch_shapes=[
            pltpu.VMEM((ROWS, FRONT + PIXELS), BF16),
            pltpu.VMEM((C3 * 16, HIDDEN), BF16),
            pltpu.VMEM((ROWS, 17 * PITCH), BF16),
            pltpu.VMEM((ROWS, 9 * PITCH), BF16),
            pltpu.VMEM((ROWS, C3 * 16), BF16),
            pltpu.VMEM((3, 16, C1), F32),
            pltpu.VMEM((2, 256, 512), BF16),
            pltpu.VMEM((2, 768, 256), BF16),
            pltpu.VMEM((2, 1152, 256), BF16),
            pltpu.VMEM((2, 768, 256), BF16),
            pltpu.VMEM((2, 1152, 256), BF16),
            pltpu.VMEM((3, NCOMP, ROWS), F32),
            pltpu.VMEM((EDGE_ROWS, ROWS), F32),
            pltpu.VMEM((2 * NBIN, ROWS), BF16),
            pltpu.SemaphoreType.DMA((2,)),
        ],
        compiler_params=pltpu.CompilerParams(vmem_limit_bytes=62 * 1024 * 1024),
        cost_estimate=pl.CostEstimate(
            flops=20_000_000_000, bytes_accessed=13_000_000, transcendentals=4_300_000
        ),
        name="owner",
    )(counts, dest.reshape(1, ROWS), pixel_ids.reshape(1, ROWS), stamps, conv1_w, conv2_w, conv3_w,
      dense_w, head_w)


def worker_kernel(got_ref, rows_ref, map_ref, coef_s, last_s):
    def add(i, total):
        part = got_ref[pl.ds(i * 8, 8), 0:MAP_ROWS, :].astype(F32)
        return total + jnp.sum(part, axis=0)

    total = lax.fori_loop(0, DEVICES // 8, add, jnp.zeros((MAP_ROWS, 128), F32))
    map_ref[pl.ds(0, PIX_DEV // 2, stride=2), :] = total[:, 0:64]
    map_ref[pl.ds(1, PIX_DEV // 2, stride=2), :] = total[:, 64:128]

    slots = DEVICES * CAP
    packed = got_ref[:, MAP_ROWS:BLOCK, :].astype(F32).reshape(slots, 128)
    head = packed + pltpu.roll(packed, 80, 1)
    live = packed[:, 96:97]
    lane = iota((slots, 128), 1)
    share = jnp.maximum(head, 0.0) + jnp.log1p(jnp.exp(-jnp.abs(head))) + 0.1
    share = jnp.where(lane < NCOMP, share, 0.0)
    share = share * (0.5 * live / jnp.sum(share, axis=1, keepdims=True))
    gate = jax.nn.sigmoid(head)
    centre = Z_TOP * pltpu.roll(gate, 112, 1)
    inverse = 1.0 / ((SPREAD_LOW + SPREAD_RANGE * pltpu.roll(gate, 96, 1)) * math.sqrt(2.0))
    coef_s[0] = share
    coef_s[1] = centre
    coef_s[2] = inverse
    last_s[...] = jnp.broadcast_to(
        jnp.sum(share * lax.erf((Z_TOP - centre) * inverse), axis=1, keepdims=True), (slots, 128)
    )
    high = 32

    def mix(step, carry):
        rows = pl.ds(pl.multiple_of(step * high, high), high)
        edge = iota((high, NBIN), 1).astype(F32) * Z_TOP / NBIN
        share, centre, inverse = coef_s[0, rows, :], coef_s[1, rows, :], coef_s[2, rows, :]
        total = jnp.zeros((high, NBIN), F32)
        for k in range(NCOMP):
            scaled = (edge - centre[:, k : k + 1]) * inverse[:, k : k + 1]
            total = total + share[:, k : k + 1] * lax.erf(scaled)
        after = pltpu.roll(total, NBIN - 1, 1)
        after = jnp.where(iota((high, NBIN), 1) == NBIN - 1, last_s[rows, 0:1], after)
        rows_ref[rows, :] = (after - total).astype(BF16)
        return carry

    lax.fori_loop(0, slots // high, mix, 0)


def worker(received):
    vmem = pl.BlockSpec(memory_space=pltpu.VMEM)
    slots = DEVICES * CAP
    return pl.pallas_call(
        worker_kernel,
        out_shape=(
            jax.ShapeDtypeStruct((slots, NBIN), BF16),
            jax.ShapeDtypeStruct((PIX_DEV, BIN_DEV), F32),
        ),
        in_specs=[vmem],
        out_specs=(vmem, vmem),
        scratch_shapes=[pltpu.VMEM((3, slots, 128), F32), pltpu.VMEM((slots, 128), F32)],
        compiler_params=pltpu.CompilerParams(vmem_limit_bytes=32 * 1024 * 1024),
        name="worker",
    )(received)


def local(*arrays):
    send = owner(*arrays)
    received = lax.all_to_all(send, ("sky", "zb"), split_axis=0, concat_axis=0, tiled=True)
    return worker(received)


def solution(mesh):
    in_specs = (
        P(("sky", "zb"), None),
        P(("sky", "zb")),
        P(("sky", "zb"), None),
        P(("sky", "zb")),
        P(),
        P(),
        P(),
        P(),
        P(),
    )
    out_specs = (P(("sky", "zb"), None), P("sky", "zb"))
    return jax.shard_map(local, mesh=mesh, in_specs=in_specs, out_specs=out_specs, check_vma=False)
```

time: 114 us -> 90.2 us (0.79)
  Pallas kernels: 0 us -> 52.1 us
  matrix products: 35.5 us -> 0 us
  local copies, waits for them, and re-layouts: 22.1 us -> 2.89 us
  other arithmetic: 12.2 us -> 0 us
  blocking collectives: 41.8 us -> 33.7 us
    pallas_call x0 -> x2, Pallas kernels: none -> 52.1 us  [the longest x1 37.3 us: owner(): pl.pallas_call(owner_kernel, out_shape=jax.ShapeDtypeStruct((DEVICES, BLO...]
    conv_general_dilated x2 -> x0, matrix products: 27.9 us -> none  [convolve(): lax.conv_general_dilated(images, kernel, (2, 2), ((1, 1), (1, 1)), dimens...]
    reshape x4 -> x0, local copies, waits for them, and re-layouts: 13.1 us -> none  [the longest x1 10.7 us: network(): stamp_grid = images.reshape(amount, STAMP, STAMP, BANDS)]
    all_to_all x1, blocking collectives: 41.8 us -> 33.7 us  [local(): lax.all_to_all(send, ('sky', 'zb'), split_axis=0, concat_axis=0, tiled=True)]
    reduce_sum x4 -> x0, other arithmetic: 7.65 us -> none  [the longest x1 7.13 us: mixture(): return jnp.sum(shares[:, :, None] * masses, axis=1)]
    dot_general x3 -> x0, matrix products: 7.54 us -> none  [the longest x1 6 us: network(): head_out = jnp.dot(hidden, head_w, preferred_element_type=jnp.float32)]
    unnamed x17 -> x2, local copies, waits for them, and re-layouts: 8.52 us -> 2.89 us
    mul x1 -> x0, other arithmetic: 3.86 us -> none  [mixture(): cumulative = 0.5 * (1.0 + lax.erf(scaled))]
where the time goes in v2:
time: 90.2 us; the launch traced here: 89.9 us
  Pallas kernels  52.1 us (58%)
  blocking collectives  33.7 us (37%)
  local copies, waits for them, and re-layouts  2.89 us (3%)
  between operations  1.29 us (1%)
    pallas_call x1, Pallas kernels, owner(): pl.pallas_call(owner_kernel, out_shape=jax.ShapeDtypeStruct((DEVICES, BLO...  37.3 us
    all_to_all x1, blocking collectives, local(): lax.all_to_all(send, ('sky', 'zb'), split_axis=0, concat_axis=0, tiled=True)  33.7 us
    pallas_call x1, Pallas kernels, worker(): pl.pallas_call(worker_kernel, out_shape=(jax.ShapeDtypeStruct((slots, NBI...  14.8 us
    unnamed x2, local copies, waits for them, and re-layouts  2.89 us

profile of v2, /device:TPU:1, one launch (start us, length us, event | category | flops | bytes accessed | tf_op | source)
XLA Modules:
  0.0 89.9 jit_solution(5065464915532279778)
XLA Ops:
  1.3 1.3 %copy.11.w1_ref = bf16[3,3,5,64]{3,2,1,0:T(8,128)(2,1)} copy(bf16[3,3,5,64]{3,1,2,0:T(4,128)(2,1)} %param.13) | data formatting | bytes 11520 | tf_op args[4]
  2.6 1.6 %copy.12.wh_ref = bf16[512,48]{1,0:T(8,128)(2,1)} copy(bf16[512,48]{0,1:T(8,128)(2,1)} %param.17) | data formatting | bytes 98304 | tf_op args[8]
  4.2 37.3 %owner.1 = bf16[128,40,128]{2,1,0:T(8,128)(2,1)} custom-call(s32[1]{0:T(128)S(6)} %copy.13.counts_ref, s32[1,512]{1,0:T(1,128)} %bitcast.2, s32[1,512]{1,0:T(1,128)} %bitcast.3, bf16[512,5120]{1,0:T(8,128)(2,1)} %x_hbm.1, bf16[3,3,5,64]{3,2,1,0:T(8,128)(2,1)} %copy.11.w1_ref, bf16[3,3,32,128]{3,2,1,0:T(8,128)(2,1)} %w2_ref.1, ...), custom_call_target="tpu_custom_call" | custom-call | flops 20000000000 | bytes 13000000 | tf_op jit(solution)/shard_map/owner/pallas_call | solution.py:267
  41.5 33.7 %all_to_all.5.got_ref = bf16[128,40,128]{2,1,0:T(8,128)(2,1)S(1)} all-to-all(bf16[128,40,128]{2,1,0:T(8,128)(2,1)} %owner.1), channel_id=1, replica_groups=mesh['sky'=16,'zb'=8] {'sky','zb'}, dimensions={0} | all-to-all | bytes 2621440 | tf_op jit(solution)/shard_map/all_to_all | solution.py:361
  75.1 14.8 %worker.1 = (bf16[1024,512]{1,0:T(8,128)(2,1)}, f32[64,64]{1,0:T(8,128)}) custom-call(bf16[128,40,128]{2,1,0:T(8,128)(2,1)S(1)} %all_to_all.5.got_ref), custom_call_target="tpu_custom_call" | custom-call | tf_op jit(solution)/shard_map/worker/pallas_call | solution.py:345

commit v3 on v2

--- a/solution.py
+++ b/solution.py
@@ -21,6 +21,7 @@
 HIDDEN = 512
 CAP = 8
 DEVICES = 128
+SLOTS = DEVICES * CAP
 SKY = 16
 ZB = 8
 PIX_DEV = NPIX // SKY
@@ -31,6 +32,8 @@
 PITCH = 1024
 EDGE_ROWS = 520
 
+FIRST, SECOND, THIRD = 2, 2, 2
+
 Z_TOP = 3.0
 SPREAD_LOW = 0.05
 SPREAD_RANGE = 0.25
@@ -59,7 +62,7 @@
     w1_s[...] = jnp.zeros_like(w1_s)
     for kh in range(3):
         for kw in range(3):
-            w1_s[kw, pl.ds(kh * BANDS, BANDS), :] = w1_ref[kh, kw].astype(F32)
+            w1_s[kw, pl.ds(kh * BANDS, BANDS), :] = w1_ref[kh, :, kw].astype(F32)
     chan, lane = iota((C1, 512), 0), iota((C1, 512), 1)
     repeat = (chan == (lane >= 256) * 32 + (lane & 31)).astype(F32).astype(BF16)
 
@@ -83,8 +86,6 @@
 
 
 def spread_second(w2_ref, w2a_s, w2b_s):
-    w2a_s[...] = jnp.zeros_like(w2a_s)
-    w2b_s[...] = jnp.zeros_like(w2b_s)
     low = iota((32, 128), 1) < 64
     zero = jnp.zeros((32, 128), F32)
     for kh in range(3):
@@ -108,8 +109,6 @@
 
 
 def spread_third(w3_ref, w3a_s, w3b_s):
-    w3a_s[...] = jnp.zeros_like(w3a_s)
-    w3b_s[...] = jnp.zeros_like(w3b_s)
     for kh in range(3):
         for kw in range(3):
             for g in range(2):
@@ -123,23 +122,52 @@
                         w3a_s[g, at : at + 64, 128 * oc : 128 * oc + 128] = tap
 
 
-def grouped(source, row, wa_s, wb_s, store):
+def grouped(source, first_row, count, wa_s, wb_s, store):
     for g in range(2):
         for half in range(2):
             width = 384 if half else 256
-            parts = []
-            for kh in range(3):
-                at = pl.multiple_of((2 * row + kh) * PITCH, PITCH) + (g * 512 + half * 128)
-                parts.append(source[:, pl.ds(pl.multiple_of(at, 128), width)])
-            weights = wb_s[g] if half else wa_s[g]
-            store(g, half, relu16(dot(jnp.concatenate(parts, axis=1), weights)))
-
-
-def coefficients(logits, mids, widths, axis, live):
-    share = jnp.maximum(logits, 0.0) + jnp.log1p(jnp.exp(-jnp.abs(logits))) + 0.1
-    return share, Z_TOP * jax.nn.sigmoid(mids), 1.0 / (
-        (SPREAD_LOW + SPREAD_RANGE * jax.nn.sigmoid(widths)) * math.sqrt(2.0)
-    )
+            stack = []
+            for i in range(count):
+                parts = []
+                for kh in range(3):
+                    at = pl.multiple_of((2 * (first_row + i) + kh) * PITCH, PITCH)
+                    at = pl.multiple_of(at + (g * 512 + half * 128), 128)
+                    parts.append(source[:, pl.ds(at, width)])
+                stack.append(jnp.concatenate(parts, axis=1))
+            out = relu16(dot(jnp.concatenate(stack, axis=0), wb_s[g] if half else wa_s[g]))
+            for i in range(count):
+                store(first_row + i, g, half, out[i * ROWS : (i + 1) * ROWS])
+
+
+def coefficients(head, live, coef_s):
+    share = jax.nn.softplus(head[0:NCOMP]) + 0.1
+    coef_s[0] = share * (0.5 * live / jnp.sum(share, axis=0, keepdims=True))
+    coef_s[1] = Z_TOP * jax.nn.sigmoid(head[NCOMP : 2 * NCOMP])
+    spread = SPREAD_LOW + SPREAD_RANGE * jax.nn.sigmoid(head[2 * NCOMP : 3 * NCOMP])
+    coef_s[2] = 1.0 / (spread * math.sqrt(2.0))
+
+
+def cumulate(coef_s, cdf_s, across):
+    blocks = 5
+    depth = EDGE_ROWS // blocks
+
+    def mix(step, carry):
+        rows = pl.multiple_of((step % blocks) * depth, 8)
+        lanes = pl.ds(pl.multiple_of((step // blocks) * 128, 128), 128)
+        edge = (iota((8, 128), 0) + rows).astype(F32) * (Z_TOP / NBIN)
+        total = [jnp.zeros((8, 128), F32)] * (depth // 8)
+        for k in range(NCOMP):
+            inverse = coef_s[2, k : k + 1, lanes]
+            scaled = (edge - coef_s[1, k : k + 1, lanes]) * inverse
+            rise = jnp.broadcast_to(inverse * (8 * Z_TOP / NBIN), (8, 128))
+            half = coef_s[0, k : k + 1, lanes]
+            for i in range(depth // 8):
+                total[i] = total[i] + half * lax.erf(scaled)
+                scaled = scaled + rise
+        cdf_s[pl.ds(rows, depth), lanes] = jnp.concatenate(total, axis=0)
+        return carry
+
+    lax.fori_loop(0, blocks * (across // 128), mix, 0)
 
 
 def owner_kernel(
@@ -152,58 +180,74 @@
     x_copy.start()
     d_copy = pltpu.make_async_copy(wd_hbm, wd_s, sems.at[1])
     d_copy.start()
-    x_s[:, 0:FRONT] = jnp.zeros((ROWS, FRONT), BF16)
-    l1_s[:, 0:PITCH] = jnp.zeros((ROWS, PITCH), BF16)
-    l2_s[:, 0:PITCH] = jnp.zeros((ROWS, PITCH), BF16)
+
+    def clear(i, carry):
+        rows = pl.ds(pl.multiple_of(i * 32, 32), 32)
+        x_s[rows, 0:FRONT] = jnp.zeros((32, FRONT), BF16)
+        l1_s[rows, 0:PITCH] = jnp.zeros((32, PITCH), BF16)
+        l2_s[rows, 0:PITCH] = jnp.zeros((32, PITCH), BF16)
+        return carry
+
+    lax.fori_loop(0, ROWS // 32, clear, 0)
+
+    def clear_weights(i, carry):
+        for g in range(2):
+            for wide in (w2b_s, w3b_s):
+                wide[g, pl.ds(pl.multiple_of(i * 48, 48), 48), :] = jnp.zeros((48, 256), BF16)
+            for narrow in (w2a_s, w3a_s):
+                narrow[g, pl.ds(pl.multiple_of(i * 32, 32), 32), :] = jnp.zeros((32, 256), BF16)
+        return carry
+
+    lax.fori_loop(0, 24, clear_weights, 0)
     spread_first(w1_ref, w1_s, t1_s)
     spread_second(w2_ref, w2a_s, w2b_s)
     spread_third(w3_ref, w3a_s, w3b_s)
     x_copy.wait()
 
-    def first(t, carry):
-        x = x_s[:, pl.ds(pl.multiple_of(t * 640, 128), 896)]
-        for odd in range(2):
-            for half in range(2):
-                start = 91 + 320 * odd + 80 * half
-                window = jnp.concatenate(
-                    [x[:, start + 160 * kh : start + 160 * kh + 85] for kh in range(3)]
-                    + [jnp.zeros((ROWS, 1), BF16)],
-                    axis=1,
-                )
-                out = relu16(dot(window, t1_s[half]))
-                at = pl.multiple_of((2 * t + odd + 1) * PITCH, PITCH)
+    def first(step, carry):
+        for half in range(2):
+            stack = []
+            for i in range(FIRST):
+                lanes = pl.ds(pl.multiple_of((step * FIRST + i) * 640, 128), 896)
+                x = x_s[:, lanes]
+                for odd in range(2):
+                    start = 91 + 320 * odd + 80 * half
+                    taps = [x[:, start + 160 * kh : start + 160 * kh + 85] for kh in range(3)]
+                    stack.append(jnp.concatenate(taps + [jnp.zeros((ROWS, 1), BF16)], axis=1))
+            out = relu16(dot(jnp.concatenate(stack, axis=0), t1_s[half]))
+            for i in range(2 * FIRST):
+                at = pl.multiple_of((2 * FIRST * step + i + 1) * PITCH, PITCH)
                 for g in range(2):
-                    l1_s[:, pl.ds(pl.multiple_of(at + (g * 512 + half * 256), 128), 256)] = out[
-                        :, g * 256 : g * 256 + 256
-                    ]
-        return carry
-
-    lax.fori_loop(0, STAMP // 4, first, 0)
-
-    def second(r, carry):
-        def store(g, half, out):
+                    lanes = pl.ds(pl.multiple_of(at + (g * 512 + half * 256), 128), 256)
+                    l1_s[:, lanes] = out[i * ROWS : (i + 1) * ROWS, g * 256 : g * 256 + 256]
+        return carry
+
+    lax.fori_loop(0, STAMP // 4 // FIRST, first, 0)
+
+    def second(step, carry):
+        def store(r, g, half, out):
             at = pl.multiple_of((r + 1) * PITCH, PITCH) + (g * 512 + half * 256)
             l2_s[:, pl.ds(pl.multiple_of(at, 128), 256)] = out
 
-        grouped(l1_s, r, w2a_s, w2b_s, store)
-        return carry
-
-    lax.fori_loop(0, STAMP // 4, second, 0)
-
-    def third(r, carry):
-        def store(g, half, out):
+        grouped(l1_s, step * SECOND, SECOND, w2a_s, w2b_s, store)
+        return carry
+
+    lax.fori_loop(0, STAMP // 4 // SECOND, second, 0)
+
+    def third(step, carry):
+        def store(r, g, half, out):
             for oc in range(2):
                 at = pl.multiple_of(r * 1024, 1024) + ((2 * half + oc) * 256 + g * 128)
                 l3_s[:, pl.ds(pl.multiple_of(at, 128), 128)] = out[:, oc * 128 : oc * 128 + 128]
 
-        grouped(l2_s, r, w3a_s, w3b_s, store)
-        return carry
-
-    lax.fori_loop(0, STAMP // 8, third, 0)
+        grouped(l2_s, step * THIRD, THIRD, w3a_s, w3b_s, store)
+        return carry
+
+    lax.fori_loop(0, STAMP // 8 // THIRD, third, 0)
     d_copy.wait()
     hidden = relu16(dot(l3_s[...], wd_s[...]))
     wh = wh_ref[...]
-    head = dot(hidden, jnp.concatenate([wh, wh, jnp.zeros((HIDDEN, 32), BF16)], axis=1))
+    head = dot_nt(hidden, jnp.concatenate([wh, wh, jnp.zeros((32, HIDDEN), BF16)], axis=0))
 
     count = counts_ref[0]
     high = head.astype(BF16).astype(F32)
@@ -220,29 +264,9 @@
     slots = dot(place, params).reshape(DEVICES, CAP, 128)
     send_ref[:, MAP_ROWS:BLOCK, :] = slots.astype(BF16)
 
-    turned = head.T
-    share, centre, inverse = coefficients(
-        turned[0:16], turned[16:32], turned[32:48], 0, None
-    )
     live = (iota((1, ROWS), 1) < count).astype(F32)
-    coef_s[0] = share * (0.5 * live / jnp.sum(share, axis=0, keepdims=True))
-    coef_s[1] = centre
-    coef_s[2] = inverse
-    blocks, depth = 5, EDGE_ROWS // 5
-
-    def mix(step, carry):
-        block, tile = step // 4, step % 4
-        lanes = pl.ds(pl.multiple_of(tile * 128, 128), 128)
-        rows = pl.multiple_of(block * depth, 8)
-        edge = (iota((depth, 128), 0) + rows).astype(F32) * Z_TOP / NBIN
-        total = jnp.zeros((depth, 128), F32)
-        for k in range(NCOMP):
-            scaled = (edge - coef_s[1, k : k + 1, lanes]) * coef_s[2, k : k + 1, lanes]
-            total = total + coef_s[0, k : k + 1, lanes] * lax.erf(scaled)
-        cdf_s[pl.ds(rows, depth), lanes] = total
-        return carry
-
-    lax.fori_loop(0, blocks * 4, mix, 0)
+    coefficients(head.T, live, coef_s)
+    cumulate(coef_s, cdf_s, ROWS)
     density = (cdf_s[1 : NBIN + 1, :] - cdf_s[0:NBIN, :]).astype(BF16).astype(F32)
 
     pixel = pixel_ref[...]
@@ -291,11 +315,12 @@
             flops=20_000_000_000, bytes_accessed=13_000_000, transcendentals=4_300_000
         ),
         name="owner",
-    )(counts, dest.reshape(1, ROWS), pixel_ids.reshape(1, ROWS), stamps, conv1_w, conv2_w, conv3_w,
-      dense_w, head_w)
-
-
-def worker_kernel(got_ref, rows_ref, map_ref, coef_s, last_s):
+    )(counts, dest.reshape(1, ROWS), pixel_ids.reshape(1, ROWS), stamps,
+      conv1_w.transpose(0, 2, 1, 3), conv2_w, conv3_w,
+      dense_w, head_w.T)
+
+
+def worker_kernel(got_ref, rows_ref, map_ref, coef_s, cdf_s):
     def add(i, total):
         part = got_ref[pl.ds(i * 8, 8), 0:MAP_ROWS, :].astype(F32)
         return total + jnp.sum(part, axis=0)
@@ -304,53 +329,26 @@
     map_ref[pl.ds(0, PIX_DEV // 2, stride=2), :] = total[:, 0:64]
     map_ref[pl.ds(1, PIX_DEV // 2, stride=2), :] = total[:, 64:128]
 
-    slots = DEVICES * CAP
-    packed = got_ref[:, MAP_ROWS:BLOCK, :].astype(F32).reshape(slots, 128)
-    head = packed + pltpu.roll(packed, 80, 1)
-    live = packed[:, 96:97]
-    lane = iota((slots, 128), 1)
-    share = jnp.maximum(head, 0.0) + jnp.log1p(jnp.exp(-jnp.abs(head))) + 0.1
-    share = jnp.where(lane < NCOMP, share, 0.0)
-    share = share * (0.5 * live / jnp.sum(share, axis=1, keepdims=True))
-    gate = jax.nn.sigmoid(head)
-    centre = Z_TOP * pltpu.roll(gate, 112, 1)
-    inverse = 1.0 / ((SPREAD_LOW + SPREAD_RANGE * pltpu.roll(gate, 96, 1)) * math.sqrt(2.0))
-    coef_s[0] = share
-    coef_s[1] = centre
-    coef_s[2] = inverse
-    last_s[...] = jnp.broadcast_to(
-        jnp.sum(share * lax.erf((Z_TOP - centre) * inverse), axis=1, keepdims=True), (slots, 128)
-    )
-    high = 32
-
-    def mix(step, carry):
-        rows = pl.ds(pl.multiple_of(step * high, high), high)
-        edge = iota((high, NBIN), 1).astype(F32) * Z_TOP / NBIN
-        share, centre, inverse = coef_s[0, rows, :], coef_s[1, rows, :], coef_s[2, rows, :]
-        total = jnp.zeros((high, NBIN), F32)
-        for k in range(NCOMP):
-            scaled = (edge - centre[:, k : k + 1]) * inverse[:, k : k + 1]
-            total = total + share[:, k : k + 1] * lax.erf(scaled)
-        after = pltpu.roll(total, NBIN - 1, 1)
-        after = jnp.where(iota((high, NBIN), 1) == NBIN - 1, last_s[rows, 0:1], after)
-        rows_ref[rows, :] = (after - total).astype(BF16)
-        return carry
-
-    lax.fori_loop(0, slots // high, mix, 0)
+    packed = got_ref[:, MAP_ROWS:BLOCK, :].astype(F32).reshape(SLOTS, 128).T
+    coefficients(packed[0:48] + packed[48:96], packed[96:97], coef_s)
+    cumulate(coef_s, cdf_s, SLOTS)
+    same = (iota((256, 256), 0) == iota((256, 256), 1)).astype(F32).astype(BF16)
+    for at in range(0, SLOTS, 256):
+        part = cdf_s[1 : NBIN + 1, at : at + 256] - cdf_s[0:NBIN, at : at + 256]
+        rows_ref[at : at + 256, :] = dot_nt(same, part.astype(BF16)).astype(BF16)
 
 
 def worker(received):
     vmem = pl.BlockSpec(memory_space=pltpu.VMEM)
-    slots = DEVICES * CAP
     return pl.pallas_call(
         worker_kernel,
         out_shape=(
-            jax.ShapeDtypeStruct((slots, NBIN), BF16),
+            jax.ShapeDtypeStruct((SLOTS, NBIN), BF16),
             jax.ShapeDtypeStruct((PIX_DEV, BIN_DEV), F32),
         ),
         in_specs=[vmem],
         out_specs=(vmem, vmem),
-        scratch_shapes=[pltpu.VMEM((3, slots, 128), F32), pltpu.VMEM((slots, 128), F32)],
+        scratch_shapes=[pltpu.VMEM((3, NCOMP, SLOTS), F32), pltpu.VMEM((EDGE_ROWS, SLOTS), F32)],
         compiler_params=pltpu.CompilerParams(vmem_limit_bytes=32 * 1024 * 1024),
         name="worker",
     )(received)

time: 90.2 us -> 77.3 us (0.86)
  Pallas kernels: 52.1 us -> 42.2 us
  local copies, waits for them, and re-layouts: 2.89 us -> 0 us
    pallas_call x1, Pallas kernels: 14.8 us -> 7.59 us  [worker(): pl.pallas_call(worker_kernel, out_shape=(jax.ShapeDtypeStruct((SLOTS, NBI...]
    unnamed x2 -> x0, local copies, waits for them, and re-layouts: 2.89 us -> none
    pallas_call x1, Pallas kernels: 37.3 us -> 34.6 us  [owner(): pl.pallas_call(owner_kernel, out_shape=jax.ShapeDtypeStruct((DEVICES, BLO...]
where the time goes in v3:
time: 77.3 us; the launch traced here: 77.1 us
  Pallas kernels  42.2 us (55%)
  blocking collectives  33.7 us (44%)
  between operations  1.29 us (2%)
    pallas_call x1, Pallas kernels, owner(): pl.pallas_call(owner_kernel, out_shape=jax.ShapeDtypeStruct((DEVICES, BLO...  34.6 us
    all_to_all x1, blocking collectives, local(): lax.all_to_all(send, ('sky', 'zb'), split_axis=0, concat_axis=0, tiled=True)  33.7 us
    pallas_call x1, Pallas kernels, worker(): pl.pallas_call(worker_kernel, out_shape=(jax.ShapeDtypeStruct((SLOTS, NBI...  7.59 us

profile of v3, /device:TPU:1, one launch (start us, length us, event | category | flops | bytes accessed | tf_op | source)
XLA Modules:
  0.0 77.1 jit_solution(8892381311994102626)
XLA Ops:
  1.3 34.6 %owner.1 = bf16[128,40,128]{2,1,0:T(8,128)(2,1)} custom-call(s32[1]{0:T(128)S(6)} %copy.11.counts_ref, s32[1,512]{1,0:T(1,128)} %bitcast.6, s32[1,512]{1,0:T(1,128)} %bitcast.7, bf16[512,5120]{1,0:T(8,128)(2,1)} %x_hbm.1, bf16[3,5,3,64]{3,2,1,0:T(4,128)(2,1)} %bitcast.5, bf16[3,3,32,128]{3,2,1,0:T(8,128)(2,1)} %w2_ref.1, bf16[3,3,64,256]{3,2,1,0:T(8,128)(2,1)} %w3_ref.1, ...), custom_call_target="tpu_custom_call" | custom-call | flops 20000000000 | bytes 13000000 | tf_op jit(solution)/shard_map/owner/pallas_call | solution.py:291
  35.8 33.7 %all_to_all.5.got_ref = bf16[128,40,128]{2,1,0:T(8,128)(2,1)S(1)} all-to-all(bf16[128,40,128]{2,1,0:T(8,128)(2,1)} %owner.1), channel_id=1, replica_groups=mesh['sky'=16,'zb'=8] {'sky','zb'}, dimensions={0} | all-to-all | bytes 2621440 | tf_op jit(solution)/shard_map/all_to_all | solution.py:359
  69.5 7.6 %worker.1 = (bf16[1024,512]{1,0:T(8,128)(2,1)}, f32[64,64]{1,0:T(8,128)}) custom-call(bf16[128,40,128]{2,1,0:T(8,128)(2,1)S(1)} %all_to_all.5.got_ref), custom_call_target="tpu_custom_call" | custom-call | tf_op jit(solution)/shard_map/worker/pallas_call | solution.py:343

commit v4 on v3

--- a/solution.py
+++ b/solution.py
@@ -33,6 +33,7 @@
 EDGE_ROWS = 520
 
 FIRST, SECOND, THIRD = 2, 2, 2
+CHUNK = 640 * FIRST
 
 Z_TOP = 3.0
 SPREAD_LOW = 0.05
@@ -85,7 +86,7 @@
     t1_s[0] = jnp.where(col == 0, 0.0, total).astype(BF16)
 
 
-def spread_second(w2_ref, w2a_s, w2b_s):
+def spread_second(w2_ref, w2_s):
     low = iota((32, 128), 1) < 64
     zero = jnp.zeros((32, 128), F32)
     for kh in range(3):
@@ -100,41 +101,61 @@
                 tile = jnp.where(low, first, second).astype(BF16)
                 for q in range(2):
                     c = d + 4 * q
-                    if -1 <= c <= 7:
-                        at = kh * 384 + 128 + 32 * c
-                        w2b_s[g, at : at + 32, 128 * q : 128 * q + 128] = tile
-                    if 0 <= c <= 7:
-                        at = kh * 256 + 32 * c
-                        w2a_s[g, at : at + 32, 128 * q : 128 * q + 128] = tile
-
-
-def spread_third(w3_ref, w3a_s, w3b_s):
+                    at = 128 + kh * 256 + 32 * c if c >= 0 else 96 - 32 * kh
+                    if c <= 7:
+                        w2_s[g, at : at + 32, 128 * q : 128 * q + 128] = tile
+
+
+def spread_third(w3_ref, w3_s):
     for kh in range(3):
         for kw in range(3):
             for g in range(2):
                 tap = w3_ref[kh, kw, :, g * 128 : g * 128 + 128]
                 for oc in range(2):
                     c = kw + 2 * oc - 1
-                    at = kh * 384 + 128 + 64 * c
-                    w3b_s[g, at : at + 64, 128 * oc : 128 * oc + 128] = tap
-                    if c >= 0:
-                        at = kh * 256 + 64 * c
-                        w3a_s[g, at : at + 64, 128 * oc : 128 * oc + 128] = tap
-
-
-def grouped(source, first_row, count, wa_s, wb_s, store):
+                    at = 256 + kh * 256 + 64 * c if c >= 0 else (64, 0, 192)[kh]
+                    w3_s[g, at : at + 64, 128 * oc : 128 * oc + 128] = tap
+
+
+def edge_second(tiles):
+    lane = iota(tiles[0].shape, 1)
+    last = jnp.where(lane >= 64, pltpu.roll(tiles[1], 96, 1), pltpu.roll(tiles[2], 64, 1))
+    return [jnp.where(lane >= 96, tiles[0], last)]
+
+
+def edge_third(tiles):
+    lane = iota(tiles[0].shape, 1)
+    return [jnp.where(lane >= 64, tiles[0], pltpu.roll(tiles[1], 64, 1)), tiles[2]]
+
+
+def grouped(source, first_row, count, edge, w_s, store):
+    ahead = w_s.shape[1] - 768
     for g in range(2):
         for half in range(2):
-            width = 384 if half else 256
             stack = []
             for i in range(count):
-                parts = []
+                parts, tiles = [], []
                 for kh in range(3):
                     at = pl.multiple_of((2 * (first_row + i) + kh) * PITCH, PITCH)
-                    at = pl.multiple_of(at + (g * 512 + half * 128), 128)
-                    parts.append(source[:, pl.ds(at, width)])
-                stack.append(jnp.concatenate(parts, axis=1))
-            out = relu16(dot(jnp.concatenate(stack, axis=0), wb_s[g] if half else wa_s[g]))
+                    at = pl.multiple_of(at + (g * 512 + half * 256), 128)
+                    parts.append(source[:, pl.ds(at, 256)])
+                    if half:
+                        tiles.append(source[:, pl.ds(pl.multiple_of(at - 128, 128), 128)])
+                if half:
+                    parts = edge(tiles) + parts
+                stack.append(parts)
+            total, at = 0.0, ahead
+            for kh in range(3):
+                piece = jnp.concatenate([parts[kh - 3] for parts in stack], axis=0)
+                total = total + dot(piece, w_s[g, at : at + 256, :])
+                at += 256
+            if half:
+                piece = jnp.concatenate(
+                    [jnp.concatenate(parts[:-3], axis=1) for parts in stack], axis=0
+                )
+                first = total[:, 0:128] + dot(piece, w_s[g, 0:ahead, 0:128])
+                total = jnp.concatenate([first, total[:, 128:256]], axis=1)
+            out = relu16(total)
             for i in range(count):
                 store(first_row + i, g, half, out[i * ROWS : (i + 1) * ROWS])
 
@@ -173,13 +194,16 @@
 def owner_kernel(
     counts_ref, dest_ref, pixel_ref, x_hbm, w1_ref, w2_ref, w3_ref, wd_hbm, wh_ref,
     send_ref,
-    x_s, wd_s, l1_s, l2_s, l3_s, w1_s, t1_s, w2a_s, w2b_s, w3a_s, w3b_s, coef_s, cdf_s, den_s,
+    x_s, wd_s, l1_s, l2_s, l3_s, w1_s, t1_s, w2_s, w3_s, coef_s, cdf_s, den_s,
     sems,
 ):
-    x_copy = pltpu.make_async_copy(x_hbm, x_s.at[:, pl.ds(FRONT, PIXELS)], sems.at[0])
-    x_copy.start()
-    d_copy = pltpu.make_async_copy(wd_hbm, wd_s, sems.at[1])
-    d_copy.start()
+    def stamps(step):
+        at = pl.multiple_of(step * CHUNK, 128)
+        to = x_s.at[:, pl.ds(pl.multiple_of(FRONT + at, 128), CHUNK)]
+        return pltpu.make_async_copy(x_hbm.at[:, pl.ds(at, CHUNK)], to, sems.at[step])
+
+    for step in range(PIXELS // CHUNK):
+        stamps(step).start()
 
     def clear(i, carry):
         rows = pl.ds(pl.multiple_of(i * 32, 32), 32)
@@ -192,19 +216,18 @@
 
     def clear_weights(i, carry):
         for g in range(2):
-            for wide in (w2b_s, w3b_s):
-                wide[g, pl.ds(pl.multiple_of(i * 48, 48), 48), :] = jnp.zeros((48, 256), BF16)
-            for narrow in (w2a_s, w3a_s):
-                narrow[g, pl.ds(pl.multiple_of(i * 32, 32), 32), :] = jnp.zeros((32, 256), BF16)
-        return carry
-
-    lax.fori_loop(0, 24, clear_weights, 0)
+            for weights in (w2_s, w3_s):
+                weights[g, pl.ds(pl.multiple_of(i * 128, 128), 128), :] = jnp.zeros((128, 256), BF16)
+        return carry
+
+    lax.fori_loop(0, 7, clear_weights, 0)
+    w3_s[:, 896:1024, :] = jnp.zeros((2, 128, 256), BF16)
     spread_first(w1_ref, w1_s, t1_s)
-    spread_second(w2_ref, w2a_s, w2b_s)
-    spread_third(w3_ref, w3a_s, w3b_s)
-    x_copy.wait()
+    spread_second(w2_ref, w2_s)
+    spread_third(w3_ref, w3_s)
 
     def first(step, carry):
+        stamps(step).wait()
         for half in range(2):
             stack = []
             for i in range(FIRST):
@@ -223,13 +246,15 @@
         return carry
 
     lax.fori_loop(0, STAMP // 4 // FIRST, first, 0)
+    d_copy = pltpu.make_async_copy(wd_hbm, wd_s, sems.at[PIXELS // CHUNK])
+    d_copy.start()
 
     def second(step, carry):
         def store(r, g, half, out):
             at = pl.multiple_of((r + 1) * PITCH, PITCH) + (g * 512 + half * 256)
             l2_s[:, pl.ds(pl.multiple_of(at, 128), 256)] = out
 
-        grouped(l1_s, step * SECOND, SECOND, w2a_s, w2b_s, store)
+        grouped(l1_s, step * SECOND, SECOND, edge_second, w2_s, store)
         return carry
 
     lax.fori_loop(0, STAMP // 4 // SECOND, second, 0)
@@ -240,7 +265,7 @@
                 at = pl.multiple_of(r * 1024, 1024) + ((2 * half + oc) * 256 + g * 128)
                 l3_s[:, pl.ds(pl.multiple_of(at, 128), 128)] = out[:, oc * 128 : oc * 128 + 128]
 
-        grouped(l2_s, step * THIRD, THIRD, w3a_s, w3b_s, store)
+        grouped(l2_s, step * THIRD, THIRD, edge_third, w3_s, store)
         return carry
 
     lax.fori_loop(0, STAMP // 8 // THIRD, third, 0)
@@ -301,14 +326,12 @@
             pltpu.VMEM((ROWS, C3 * 16), BF16),
             pltpu.VMEM((3, 16, C1), F32),
             pltpu.VMEM((2, 256, 512), BF16),
-            pltpu.VMEM((2, 768, 256), BF16),
-            pltpu.VMEM((2, 1152, 256), BF16),
-            pltpu.VMEM((2, 768, 256), BF16),
-            pltpu.VMEM((2, 1152, 256), BF16),
+            pltpu.VMEM((2, 896, 256), BF16),
+            pltpu.VMEM((2, 1024, 256), BF16),
             pltpu.VMEM((3, NCOMP, ROWS), F32),
             pltpu.VMEM((EDGE_ROWS, ROWS), F32),
             pltpu.VMEM((2 * NBIN, ROWS), BF16),
-            pltpu.SemaphoreType.DMA((2,)),
+            pltpu.SemaphoreType.DMA((PIXELS // CHUNK + 1,)),
         ],
         compiler_params=pltpu.CompilerParams(vmem_limit_bytes=62 * 1024 * 1024),
         cost_estimate=pl.CostEstimate(

time: 77.3 us -> 74.4 us (0.962)
  Pallas kernels: 42.2 us -> 39.2 us
    pallas_call x1, Pallas kernels: 34.6 us -> 31.6 us  [owner(): pl.pallas_call(owner_kernel, out_shape=jax.ShapeDtypeStruct((DEVICES, BLO...]
where the time goes in v4:
time: 74.4 us; the launch traced here: 74.2 us
  Pallas kernels  39.2 us (53%)
  blocking collectives  33.7 us (45%)
  between operations  1.29 us (2%)
    all_to_all x1, blocking collectives, local(): lax.all_to_all(send, ('sky', 'zb'), split_axis=0, concat_axis=0, tiled=True)  33.7 us
    pallas_call x1, Pallas kernels, owner(): pl.pallas_call(owner_kernel, out_shape=jax.ShapeDtypeStruct((DEVICES, BLO...  31.6 us
    pallas_call x1, Pallas kernels, worker(): pl.pallas_call(worker_kernel, out_shape=(jax.ShapeDtypeStruct((SLOTS, NBI...  7.59 us

profile of v4, /device:TPU:1, one launch (start us, length us, event | category | flops | bytes accessed | tf_op | source)
XLA Modules:
  0.0 74.2 jit_solution(12812000812103039343)
XLA Ops:
  1.3 31.6 %owner.1 = bf16[128,40,128]{2,1,0:T(8,128)(2,1)} custom-call(s32[1]{0:T(128)S(6)} %copy.11.counts_ref, s32[1,512]{1,0:T(1,128)} %bitcast.6, s32[1,512]{1,0:T(1,128)} %bitcast.7, bf16[512,5120]{1,0:T(8,128)(2,1)} %x_hbm.1, bf16[3,5,3,64]{3,2,1,0:T(4,128)(2,1)} %bitcast.5, bf16[3,3,32,128]{3,2,1,0:T(8,128)(2,1)} %w2_ref.1, bf16[3,3,64,256]{3,2,1,0:T(8,128)(2,1)} %w3_ref.1, ...), custom_call_target="tpu_custom_call" | custom-call | flops 20000000000 | bytes 13000000 | tf_op jit(solution)/shard_map/owner/pallas_call | solution.py:316
  32.9 33.7 %all_to_all.5.got_ref = bf16[128,40,128]{2,1,0:T(8,128)(2,1)S(1)} all-to-all(bf16[128,40,128]{2,1,0:T(8,128)(2,1)} %owner.1), channel_id=1, replica_groups=mesh['sky'=16,'zb'=8] {'sky','zb'}, dimensions={0} | all-to-all | bytes 2621440 | tf_op jit(solution)/shard_map/all_to_all | solution.py:382
  66.6 7.6 %worker.1 = (bf16[1024,512]{1,0:T(8,128)(2,1)}, f32[64,64]{1,0:T(8,128)}) custom-call(bf16[128,40,128]{2,1,0:T(8,128)(2,1)S(1)} %all_to_all.5.got_ref), custom_call_target="tpu_custom_call" | custom-call | tf_op jit(solution)/shard_map/worker/pallas_call | solution.py:366

commit v5 on v4

--- a/solution.py
+++ b/solution.py
@@ -30,7 +30,7 @@
 BLOCK = MAP_ROWS + CAP
 FRONT = 256
 PITCH = 1024
-EDGE_ROWS = 520
+EDGE_ROWS = 528
 
 FIRST, SECOND, THIRD = 2, 2, 2
 CHUNK = 640 * FIRST
@@ -169,7 +169,7 @@
 
 
 def cumulate(coef_s, cdf_s, across):
-    blocks = 5
+    blocks = 3
     depth = EDGE_ROWS // blocks
 
     def mix(step, carry):

time: 74.4 us -> 73.8 us (level)
  no operation moved by 1% of the time
where the time goes in v5:
time: 73.8 us; the launch traced here: 73.6 us
  Pallas kernels  38.6 us (52%)
  blocking collectives  33.7 us (46%)
  between operations  1.29 us (2%)
    all_to_all x1, blocking collectives, local(): lax.all_to_all(send, ('sky', 'zb'), split_axis=0, concat_axis=0, tiled=True)  33.7 us
    pallas_call x1, Pallas kernels, owner(): pl.pallas_call(owner_kernel, out_shape=jax.ShapeDtypeStruct((DEVICES, BLO...  31.4 us
    pallas_call x1, Pallas kernels, worker(): pl.pallas_call(worker_kernel, out_shape=(jax.ShapeDtypeStruct((SLOTS, NBI...  7.21 us

profile of v5, /device:TPU:1, one launch (start us, length us, event | category | flops | bytes accessed | tf_op | source)
XLA Modules:
  0.0 73.6 jit_solution(2938451588331245789)
XLA Ops:
  1.3 31.4 %owner.1 = bf16[128,40,128]{2,1,0:T(8,128)(2,1)} custom-call(s32[1]{0:T(128)S(6)} %copy.11.counts_ref, s32[1,512]{1,0:T(1,128)} %bitcast.6, s32[1,512]{1,0:T(1,128)} %bitcast.7, bf16[512,5120]{1,0:T(8,128)(2,1)} %x_hbm.1, bf16[3,5,3,64]{3,2,1,0:T(4,128)(2,1)} %bitcast.5, bf16[3,3,32,128]{3,2,1,0:T(8,128)(2,1)} %w2_ref.1, bf16[3,3,64,256]{3,2,1,0:T(8,128)(2,1)} %w3_ref.1, ...), custom_call_target="tpu_custom_call" | custom-call | flops 20000000000 | bytes 13000000 | tf_op jit(solution)/shard_map/owner/pallas_call | solution.py:316
  32.7 33.7 %all_to_all.5.got_ref = bf16[128,40,128]{2,1,0:T(8,128)(2,1)S(1)} all-to-all(bf16[128,40,128]{2,1,0:T(8,128)(2,1)} %owner.1), channel_id=1, replica_groups=mesh['sky'=16,'zb'=8] {'sky','zb'}, dimensions={0} | all-to-all | bytes 2621440 | tf_op jit(solution)/shard_map/all_to_all | solution.py:382
  66.4 7.2 %worker.1 = (bf16[1024,512]{1,0:T(8,128)(2,1)}, f32[64,64]{1,0:T(8,128)}) custom-call(bf16[128,40,128]{2,1,0:T(8,128)(2,1)S(1)} %all_to_all.5.got_ref), custom_call_target="tpu_custom_call" | custom-call | tf_op jit(solution)/shard_map/worker/pallas_call | solution.py:366
